TPU v7x, 256 devices: a whole 4x4x8 slice. The times are simulated.
256 devices in a mesh: seq: 64 (over z, x, core), head: 4 (over y).
Axes of the slice: x: 4, y: 4, z: 8, core: 2. Of those that a mesh axis runs over, the one named last changes fastest.
Arguments:
- queries: bfloat16 [8704, 1024], P('seq', 'head'), may hold values from -5 to 5
- key_rows: bfloat16 [8704, 1024], P('seq', 'head'), may hold values from -5 to 5
- value_rows: bfloat16 [8704, 1024], P('seq', 'head'), may hold values from -6 to 6
- scale_of: int32 [8704], P('seq'), may hold values from -1 to 12, as said below
- wo: bfloat16 [1024, 2048], P('head'), may hold values from -0.1875 to 0.1875
- dy: bfloat16 [8704, 2048], P('seq', 'head'), may hold values from -16 to 16
Outputs:
- block_out: bfloat16 [8704, 2048], P('seq', 'head')
- dq: bfloat16 [8704, 1024], P('seq', 'head')
- dk: bfloat16 [8704, 1024], P('seq', 'head')
- dv: bfloat16 [8704, 1024], P('seq', 'head')
- dwo: float32 [1024, 2048], P('head', 'seq')
Inputs may be any that keep to these rules, and one draw needn't show every extreme that they name: `scale_of`: in each aligned block of 136 rows (one index of seq) the first 128 rows hold ids 13 - 3 to 12, not falling over these rows of all blocks taken in order, each of the three ids present; the last 8 rows of a block are all -1 except in exactly 4 blocks, whose last rows hold ids 0 to 9, not falling within the block.
All inputs are finite; a program needn't handle non-finite values.
Results may differ from a plain program's by a relative error of at most 0.035.
Values may be sent and summed in bfloat16 or wider, within the bound.
No kernel may reach another device: no remote copies, remote signals or barrier semaphores. Data moves between devices by JAX's collectives and lax.ppermute only.
A program may use at most 192 MiB of HBM per device.

v0:
```python
import jax
import jax.numpy as jnp
from jax import lax
from jax.sharding import PartitionSpec as P

DH = 128


def masked_logits(q_part, k_part, q_ids, k_ids, scale):
    s = jnp.einsum("qhd,khd->hqk", q_part, k_part, preferred_element_type=jnp.float32) * scale
    seen = (k_ids[None, :] >= 0) & (k_ids[None, :] <= q_ids[:, None])
    return jnp.where(seen[None], s, -1e30)


def local(queries, key_rows, value_rows, scale_of, wo, dy):
    rows = queries.shape[0]
    feats = queries.shape[1]
    heads = feats // DH
    nseq = lax.axis_size("seq")
    scale = DH ** (-0.5)
    group = 8
    blocks = nseq // group
    width = group * rows
    q_ids = scale_of.astype(jnp.float32)
    valid = (scale_of >= 0).astype(jnp.float32)
    q_heads = queries.reshape(rows, heads, DH)
    k_all, v_all, ids_all = (
        lax.all_gather(key_rows, "seq", axis=0, tiled=True),
        lax.all_gather(value_rows, "seq", axis=0, tiled=True),
        lax.all_gather(scale_of.astype(jnp.bfloat16), "seq", axis=0, tiled=True),
    )
    k_blocks = k_all.reshape(blocks, width, heads, DH)
    v_blocks = v_all.reshape(blocks, width, heads, DH)
    id_blocks = ids_all.astype(jnp.float32).reshape(blocks, width)

    def reach(carry, items):
        top, total = carry
        k_block, id_block = items
        s = masked_logits(q_heads, k_block, q_ids, id_block, scale)
        new_top = jnp.maximum(top, jnp.max(s, axis=2))
        total = total * jnp.exp(top - new_top) + jnp.sum(jnp.exp(s - new_top[:, :, None]), axis=2)
        return ((new_top, total), None)

    start_top = jnp.full((heads, rows), -1e30, jnp.float32)
    start_total = jnp.zeros((heads, rows), jnp.float32)
    (top, total), _ = lax.scan(reach, (start_top, start_total), (k_blocks, id_blocks))
    lse = top + jnp.log(total)

    def mix(acc, items):
        k_block, v_block, id_block = items
        s = masked_logits(q_heads, k_block, q_ids, id_block, scale)
        weights = jnp.exp(s - lse[:, :, None]).astype(jnp.bfloat16)
        return (
            acc + jnp.einsum("hqk,khd->qhd", weights, v_block, preferred_element_type=jnp.float32),
            None,
        )

    out, _ = lax.scan(
        mix, jnp.zeros((rows, heads, DH), jnp.float32), (k_blocks, v_blocks, id_blocks)
    )
    attn = (out.reshape(rows, feats) * valid[:, None]).astype(jnp.bfloat16)
    partial_out = jnp.dot(attn, wo, preferred_element_type=jnp.float32)
    block_out = lax.psum_scatter(
        partial_out.astype(jnp.bfloat16), "head", scatter_dimension=1, tiled=True
    )
    dy_full = lax.all_gather(dy, "head", axis=1, tiled=True)
    dattn = (
        jnp.einsum("td,fd->tf", dy_full, wo, preferred_element_type=jnp.float32) * valid[:, None]
    ).astype(jnp.bfloat16)
    dattn_heads = dattn.reshape(rows, heads, DH)
    delta = jnp.sum(
        dattn_heads.astype(jnp.float32) * attn.reshape(rows, heads, DH).astype(jnp.float32), axis=2
    )
    delta_heads = delta.T

    def grads_query(acc, items):
        k_block, v_block, id_block = items
        s = masked_logits(q_heads, k_block, q_ids, id_block, scale)
        prob = jnp.exp(s - lse[:, :, None])
        dprob = jnp.einsum("qhd,khd->hqk", dattn_heads, v_block, preferred_element_type=jnp.float32)
        dscore = (prob * (dprob - delta_heads[:, :, None]) * scale).astype(jnp.bfloat16)
        return (
            acc + jnp.einsum("hqk,khd->qhd", dscore, k_block, preferred_element_type=jnp.float32),
            None,
        )

    dq_sum, _ = lax.scan(
        grads_query, jnp.zeros((rows, heads, DH), jnp.float32), (k_blocks, v_blocks, id_blocks)
    )
    dq = dq_sum.reshape(rows, feats).astype(jnp.bfloat16)
    dwo = lax.psum_scatter(
        jnp.einsum("tf,td->fd", attn, dy_full, preferred_element_type=jnp.float32),
        "seq",
        scatter_dimension=1,
        tiled=True,
    )
    ids_float = ids_all.astype(jnp.float32)
    count = lax.axis_size("seq") * rows
    k_part = k_all.reshape(count, heads, DH)
    v_part = v_all.reshape(count, heads, DH)
    s = masked_logits(q_heads, k_part, q_ids, ids_float, scale)
    prob = jnp.exp(s - lse[:, :, None])
    dprob = jnp.einsum("qhd,khd->hqk", dattn_heads, v_part, preferred_element_type=jnp.float32)
    dscore = (prob * (dprob - delta_heads[:, :, None]) * scale).astype(jnp.bfloat16)
    dk_term = jnp.einsum(
        "hqk,qhd->khd", dscore, q_heads, preferred_element_type=jnp.float32
    ).reshape(count, feats)
    dv_term = jnp.einsum(
        "hqk,qhd->khd", prob.astype(jnp.bfloat16), dattn_heads, preferred_element_type=jnp.float32
    ).reshape(count, feats)
    both = lax.psum_scatter(
        jnp.concatenate([dk_term, dv_term], axis=1), "seq", scatter_dimension=0, tiled=True
    )
    dk = both[:, :feats].astype(jnp.bfloat16)
    dv = both[:, feats:].astype(jnp.bfloat16)
    return (block_out, dq, dk, dv, dwo)


def solution(mesh):
    placed = (
        P("seq", "head"),
        P("seq", "head"),
        P("seq", "head"),
        P("seq"),
        P("head", None),
        P("seq", "head"),
    )
    return jax.shard_map(
        local,
        mesh=mesh,
        in_specs=placed,
        out_specs=(
            P("seq", "head"),
            P("seq", "head"),
            P("seq", "head"),
            P("seq", "head"),
            P("head", "seq"),
        ),
        check_vma=False,
    )
```

profile of v0, /device:TPU:8, one launch (start us, length us, event | category | flops | bytes accessed | tf_op | source)
XLA Modules:
  0.0 781.6 jit_solution(5077319957987343560)
XLA Ops:
  7.2 0.7 all-gather.3.cloned.1.call-update
  8.0 0.7 all-gather.5.cloned.1.call-update
  8.7 1.3 dynamic-slice
  10.7 0.8 fusion.74
  11.6 254.2 %all-reduce = bf16[8704]{0:T(1024)(128)(2,1)S(1)} all-reduce(bf16[8704]{0:T(1024)(128)(2,1)S(1)} %dynamic-update-slice), channel_id=1, replica_groups=mesh['seq'=64,'head'=4] {'seq'}, use_global_device_ids=true, to_apply=%add | all-reduce | flops 8704 | bytes 34816
  266.0 13.2 %all_gather.15 = bf16[136,2048]{1,0:T(8,128)(2,1)S(1)} all-gather(bf16[136,512]{1,0:T(8,128)(2,1)} %param.17), channel_id=1, replica_groups=mesh['seq'=64,'head'=4] {'head'}, dimensions={1}, use_global_device_ids=true | all-gather | bytes 696320 | tf_op jit(solution)/shard_map/all_gather | solution.py:66
  279.2 0.7 compare_convert_fusion
  280.4 0.9 copy_bitcast_fusion.2
  281.3 1.9 compare_and_fusion.3
  283.2 9.5 %reshape.248 = bf16[8,1088,2,128]{3,2,1,0:T(2,128)(2,1)} reshape(bf16[8704,256]{1,0:T(8,128)(2,1)} %all-gather.3.cloned.1.call-done) | data formatting | bytes 8912896 | tf_op jit(solution)/shard_map/reshape | solution.py:33
  292.7 5.2 copy.84
  297.9 9.5 %reshape.249 = bf16[8,1088,2,128]{3,2,1,0:T(2,128)(2,1)} reshape(bf16[8704,256]{1,0:T(8,128)(2,1)} %all-gather.5.cloned.1.call-done) | data formatting | bytes 8912896 | tf_op jit(solution)/shard_map/reshape | solution.py:32
  307.3 5.2 copy.85
  312.6 18.7 %while.35 = (s32[]{:T(128)}, f32[2,136]{1,0:T(2,128)S(1)}, f32[2,136]{1,0:T(2,128)S(1)}, f32[8,1088]{1,0:T(8,128)S(1)}, f32[136]{0:T(256)S(1)}, /*index=5*/bf16[...) while((s32[]{:T(128)}, f32[2,136]{1,0:T(2,128)S(1)}, ...), condition=%wide.region_3.4_spmd.clone, body=%wide.region_0.3_spmd.clone.sunk | while | flops 77537680 | bytes 3324508 | solution.py:46
  312.8 1.7 fusion.106
  315.2 1.7 fusion.106
  317.5 1.7 fusion.106
  319.9 1.7 fusion.106
  322.2 1.7 fusion.106
  324.5 1.7 fusion.106
  326.9 1.7 fusion.106
  329.2 1.7 fusion.106
  331.3 18.4 %while.36 = (s32[]{:T(128)}, f32[136,2,128]{2,0,1:T(8,128)S(1)}, bf16[8,1088,2,128]{3,1,2,0:T(8,128)(2,1)}, f32[8,1088]{1,0:T(8,128)S(1)}, f32[136]{0:T(256)S(1)...) while((s32[]{:T(128)}, f32[136,2,128]{2,0,1:T(8,128)S(1)}, ...), condition=%wide.region_5.6_spmd.clone, body=%wide.region_4.5_spmd.clone.sunk | while | flops 153069632 | bytes 1781086 | solution.py:58
  331.6 2.0 fusion.112
  333.9 2.0 fusion.112
  336.2 2.0 fusion.112
  338.5 2.0 fusion.112
  340.8 2.0 fusion.112
  343.1 2.0 fusion.112
  345.4 2.0 fusion.112
  347.7 2.0 fusion.112
  350.1 6.6 copy.96
  356.7 4.7 fusion.60
  361.5 5.5 fusion.62
  366.9 0.8 copy-done.1
  367.8 9.3 %copy.106 = f32[8704,256]{1,0:T(8,128)} copy(f32[8704,256]{0,1:T(8,128)} %bitcast.162) | data formatting | bytes 17825792 | tf_op jit(solution)/shard_map/reshape | solution.py:110
  377.1 6.6 copy.99
  383.7 11.3 %fusion.64 = f32[2,8704,128]{1,2,0:T(8,128)} fusion(f32[2,136,8704]{2,1,0:T(8,128)} %copy-done.1, bf16[8704,2,128]{0,2,1:T(8,128)(2,1)} %bitcast.163, f32[2,136]{1,0:T(2,128)S(1)} %copy.94, bf16[17,2,8,128]{3,2,1,0:T(8,128)(2,1)S(1)} %fusion.66, bf16[136,256]{1,0:T(8,128)(2,1)S(1)} %copy-done.2), kind=kOutput, calls=%fused_computation.79 | convolution fusion | flops 1221623808 | bytes 22979648 | tf_op jit(solution)/shard_map/hqk,qhd->khd/dot_general | solution.py:105
  394.9 9.3 %copy.105 = f32[8704,256]{1,0:T(8,128)} copy(f32[8704,256]{0,1:T(8,128)} %bitcast.161) | data formatting | bytes 17825792 | tf_op jit(solution)/shard_map/reshape | solution.py:107
  404.3 12.4 %pad_maximum_fusion = f32[8704,512]{1,0:T(8,128)} fusion(f32[8704,256]{1,0:T(8,128)} %copy.106, f32[8704,256]{1,0:T(8,128)} %copy.105), kind=kLoop, calls=%fused_computation.66 | loop fusion | flops 4456448 | bytes 35651584 | tf_op jit(solution)/shard_map/concatenate | solution.py:112
  416.8 1.2 convolution_convert_fusion
  418.0 2.0 fusion.69
  420.0 32.0 %while.37 = (s32[]{:T(128)}, f32[136,2,128]{2,0,1:T(8,128)S(1)}, bf16[8,1088,2,128]{3,1,2,0:T(8,128)(2,1)}, f32[8,1088]{1,0:T(8,128)S(1)}, f32[136]{0:T(256)S(1)...) while((s32[]{:T(128)}, f32[136,2,128]{2,0,1:T(8,128)S(1)}, ...), condition=%wide.region_9.10_spmd.clone, body=%wide.region_8.9_spmd.clone.sunk | while | flops 229717056 | bytes 4776370 | solution.py:87
  420.3 1.6 fusion.118
  421.9 2.1 fusion.119
  424.2 1.6 fusion.118
  425.8 2.2 fusion.119
  428.2 1.6 fusion.118
  429.8 2.2 fusion.119
  432.2 1.6 fusion.118
  433.8 2.2 fusion.119
  436.2 1.6 fusion.118
  437.8 2.2 fusion.119
  440.3 1.6 fusion.118
  441.9 2.1 fusion.119
  444.3 1.6 fusion.118
  445.9 2.2 fusion.119
  448.3 1.6 fusion.118
  449.9 2.2 fusion.119
  452.7 151.6 %reduce-scatter.10.cloned.1.call-done = f32[136,512]{1,0:T(8,128)} async-done(((f32[8704,512]{1,0:T(8,128)}), f32[136,512]{1,0:T(8,128)}) %reduce-scatter.10.cloned.1.call-update) | async-done | bytes 278544
  604.3 1.0 convert.4
  605.2 0.7 fusion.73
  605.9 22.1 %reduce-scatter.6.cloned.1.call-done = bf16[136,512]{1,0:T(8,128)(2,1)} async-done(((bf16[136,2048]{1,0:T(8,128)(2,1)}), bf16[136,512]{1,0:T(8,128)(2,1)}) %reduce-scatter.6.cloned.1.call-update) | async-done | bytes 139280 | tf_op jit(solution)/shard_map/reduce_scatter | solution.py:63
  628.0 147.0 %reduce-scatter.8.cloned.1.call-done = f32[256,32]{0,1:T(8,128)} async-done(((f32[256,2048]{0,1:T(8,128)}), f32[256,32]{0,1:T(8,128)}) %reduce-scatter.8.cloned.1.call-update) | async-done | bytes 32784 | tf_op jit(solution)/shard_map/reduce_scatter | solution.py:91
  (135 shorter events, 10.7 us)
Async XLA Ops:
  7.2 272.7 %copy-start = (bf16[256,2048]{1,0:T(8,128)(2,1)S(1)}, bf16[256,2048]{1,0:T(8,128)(2,1)}, u32[]{:S(2)}) copy-start(bf16[256,2048]{1,0:T(8,128)(2,1)} %param.16) | copy-start | bytes 3145732
  7.2 276.0 %all-gather.3.cloned.1.call-start = ((), (), s32[]{:S(2)}) async-start(), calls=%async_computation.3 | async-start | bytes 4526080 | tf_op jit(solution)/shard_map/all_gather | solution.py:29
  7.9 290.0 %all-gather.5.cloned.1.call-start = ((), (), s32[]{:S(2)}) async-start(), calls=%async_computation.4 | async-start | bytes 4526080 | tf_op jit(solution)/shard_map/all_gather | solution.py:28
  8.7 595.6 %reduce-scatter.10.cloned.1.call-start = ((), (), s32[]{:S(2)}) async-start(), calls=%async_computation.7 | async-start | bytes 18104320
  350.1 6.6 copy-start.2
  361.4 6.3 copy-start.1
  416.7 211.3 %reduce-scatter.6.cloned.1.call-start = ((), (), s32[]{:S(2)}) async-start(), calls=%async_computation.5 | async-start | bytes 696320 | tf_op jit(solution)/shard_map/reduce_scatter | solution.py:63
  418.0 357.1 %reduce-scatter.8.cloned.1.call-start = ((), (), s32[]{:S(2)}) async-start(), calls=%async_computation.6 | async-start | bytes 2129920 | tf_op jit(solution)/shard_map/reduce_scatter | solution.py:91
Sparse Core Ops, SparseCore 0:
  10.7 82.0 all-gather.2
  95.4 76.5 all-gather.4
  416.8 187.3 reduce-scatter.9
  607.4 20.5 reduce-scatter.5
  632.5 142.5 reduce-scatter.7
where the time goes:
time: 784 us; the launch traced here: 782 us
  waiting for transfers between devices  322 us (41%)
  blocking collectives  267 us (34%)
  matrix products  84.7 us (11%)
  local copies, waits for them, and re-layouts  66 us (8%)
  other arithmetic  25.5 us (3%)
  between operations  14.6 us (2%)
    unnamed x1, blocking collectives  254 us
    unnamed x6, waiting for transfers between devices  153 us
    reduce_scatter x1, waiting for transfers between devices, local(): lax.psum_scatter(jnp.einsum('tf,td->fd', attn, dy_full, preferred_element...  147 us
    reduce_scatter x1, waiting for transfers between devices, local(): lax.psum_scatter(partial_out.astype(jnp.bfloat16), 'head', scatter_dimens...  22.1 us
    dot_general x9, matrix products, masked_logits(): jnp.einsum('qhd,khd->hqk', q_part, k_part, preferred_element_type=jnp.flo...  18.3 us
    dot_general x8, matrix products, grads_query(): jnp.einsum('hqk,khd->qhd', dscore, k_block, preferred_element_type=jnp.fl...  17.2 us
    dot_general x8, matrix products, mix(): jnp.einsum('hqk,khd->qhd', weights, v_block, preferred_element_type=jnp.f...  16.2 us
  transfers between devices with their start and end apart: 5, of which 3 were waited for; matrix products, arithmetic and copies ran while one was open for 7% of the time, Pallas kernels for 0%

commit v1 on v0

v1 whole, which is shorter than its diff:
```python
import functools
import math

import jax
import jax.numpy as jnp
from jax import lax
from jax.experimental import pallas as pl
from jax.experimental.pallas import tpu as pltpu
from jax.sharding import Mesh, PartitionSpec as P

DH = 128
BIG = -1e30
SCALE = DH ** (-0.5)
UNIT = SCALE * math.log2(math.e)
F32 = jnp.float32
BF16 = jnp.bfloat16
LAST = (((1,), (1,)), ((), ()))


def forward_kernel(q_ref, qm_ref, kv_ref, km_ref, da_ref, o_ref, stat_ref):
    rows = q_ref.shape[0]
    lane = lax.broadcasted_iota(jnp.int32, (rows, DH), 1)
    stat = jnp.zeros((rows, DH), F32)
    for head in range(2):
        cols = slice(head * DH, (head + 1) * DH)
        q_ext = jnp.concatenate([q_ref[:, cols], qm_ref[...]], axis=1)
        k_ext = jnp.concatenate([kv_ref[:, cols], km_ref[...]], axis=1)
        s = lax.dot_general(q_ext, k_ext, LAST, preferred_element_type=F32)
        top = jnp.max(s, axis=1, keepdims=True)
        p = jnp.exp2((s - top) * UNIT)
        total = jnp.sum(p, axis=1, keepdims=True)
        v = kv_ref[:, 2 * DH + head * DH : 2 * DH + (head + 1) * DH]
        o = jnp.dot(p.astype(BF16), v, preferred_element_type=F32) / total
        o_ref[:, cols] = o.astype(BF16)
        lse = top * UNIT + jnp.log2(total)
        share = jnp.sum(o * da_ref[:, cols].astype(F32), axis=1, keepdims=True)
        stat = jnp.where(lane == head, lse, stat)
        stat = jnp.where(lane == 2 + head, share, stat)
    stat_ref[...] = stat.T[:8]


def backward_kernel(q_ref, qm_ref, da_ref, kv_ref, km_ref, stat_ref, dq_ref, dkv_ref, ds_ref, row_ref):
    step = pl.program_id(0)
    block = kv_ref.shape[0]

    @pl.when(step == 0)
    def _():
        stat = stat_ref[...]
        lse_each = stat[:, 0:2]
        top = jnp.max(lse_each, axis=0)
        weight = jnp.exp2(lse_each - top[None])
        total = jnp.sum(weight, axis=0)
        lse = top + jnp.log2(total)
        row_ref[0:2] = jnp.where(lse < -1e28, 1e30, lse)
        row_ref[2:4] = jnp.sum(weight * stat[:, 2:4], axis=0) / total

    for head in range(2):
        cols = slice(head * DH, (head + 1) * DH)
        vcols = slice(2 * DH + head * DH, 2 * DH + (head + 1) * DH)
        q = q_ref[:, cols]
        da = da_ref[:, cols]
        q_ext = jnp.concatenate([q, qm_ref[...]], axis=1)
        k_ext = jnp.concatenate([kv_ref[:, cols], km_ref[...]], axis=1)
        s = lax.dot_general(k_ext, q_ext, LAST, preferred_element_type=F32)
        p = jnp.exp2(s * UNIT - row_ref[head : head + 1, :])
        dp = lax.dot_general(kv_ref[:, vcols], da, LAST, preferred_element_type=F32)
        ds = (p * (dp - row_ref[2 + head : 3 + head, :])).astype(BF16)
        dkv_ref[:, vcols] = jnp.dot(p.astype(BF16), da, preferred_element_type=F32).astype(BF16)
        dkv_ref[:, cols] = (jnp.dot(ds, q, preferred_element_type=F32) * SCALE).astype(BF16)
        ds_ref[head, pl.ds(pl.multiple_of(step * block, block), block), :] = ds


def query_kernel(ds_ref, kv_ref, dq_ref):
    for head in range(2):
        cols = slice(head * DH, (head + 1) * DH)
        dq = lax.dot_general(ds_ref[head], kv_ref[:, cols], (((0,), (0,)), ((), ())), preferred_element_type=F32)
        dq_ref[:, cols] = (dq * SCALE).astype(BF16)


def backward(q_ref, qm_ref, da_ref, kv_ref, km_ref, kv_all_ref, stat_ref, dq_ref, dkv_ref, ds_ref, row_ref):
    backward_kernel(q_ref, qm_ref, da_ref, kv_ref, km_ref, stat_ref, dq_ref, dkv_ref, ds_ref, row_ref)

    @pl.when(pl.program_id(0) == pl.num_programs(0) - 1)
    def _():
        query_kernel(ds_ref, kv_all_ref, dq_ref)


def local(queries, key_rows, value_rows, scale_of, wo, dy):
    rows, feats = queries.shape
    valid = (scale_of >= 0).astype(F32)
    kv = lax.all_gather(jnp.concatenate([key_rows, value_rows], axis=1), "z", axis=0, tiled=True)
    q = lax.all_gather(queries, "xc", axis=0, tiled=True)
    q_ids = lax.all_gather(scale_of, "xc", axis=0, tiled=True)
    k_ids = lax.all_gather(scale_of, "z", axis=0, tiled=True)
    dy_full = lax.all_gather(dy, "head", axis=1, tiled=True)
    da_own = (
        jnp.einsum("td,fd->tf", dy_full, wo, preferred_element_type=F32) * valid[:, None]
    ).astype(BF16)
    da = lax.all_gather(da_own, "xc", axis=0, tiled=True)

    lane = jnp.arange(DH, dtype=jnp.int32)[None, :]
    hidden = ((lane > q_ids[:, None]) & (lane < 13)) | (lane == 13)
    qm = jnp.where(hidden, BIG, 0.0).astype(BF16)
    km = (lane == jnp.where(k_ids < 0, 13, k_ids)[:, None]).astype(BF16)

    nq, nk = q.shape[0], kv.shape[0]
    blocks = 4
    qb, kb = nq // blocks, nk // blocks
    qpad = 384

    def whole(shape):
        return pl.BlockSpec(shape, lambda i: (0,) * len(shape))

    o, stat = pl.pallas_call(
        forward_kernel,
        grid=(blocks,),
        in_specs=[
            pl.BlockSpec((qb, feats), lambda i: (i, 0)),
            pl.BlockSpec((qb, DH), lambda i: (i, 0)),
            whole((nk, 2 * feats)),
            whole((nk, DH)),
            pl.BlockSpec((qb, feats), lambda i: (i, 0)),
        ],
        out_specs=[
            pl.BlockSpec((qb, feats), lambda i: (i, 0)),
            pl.BlockSpec((None, 8, qb), lambda i: (i, 0, 0)),
        ],
        out_shape=[
            jax.ShapeDtypeStruct((nq, feats), BF16),
            jax.ShapeDtypeStruct((blocks, 8, qb), F32),
        ],
        compiler_params=pltpu.CompilerParams(vmem_limit_bytes=48 << 20),
    )(q, qm, kv, km, da)
    stat = stat[:, :4].transpose(1, 0, 2).reshape(4, nq)
    stats = lax.all_gather(stat, "xc", axis=0, tiled=False)

    dq_part, dkv_part = pl.pallas_call(
        backward,
        grid=(blocks,),
        in_specs=[
            whole((nq, feats)),
            whole((nq, DH)),
            whole((nq, feats)),
            pl.BlockSpec((kb, 2 * feats), lambda i: (i, 0)),
            pl.BlockSpec((kb, DH), lambda i: (i, 0)),
            whole((nk, 2 * feats)),
            whole(stats.shape),
        ],
        out_specs=[
            whole((nq, feats)),
            pl.BlockSpec((kb, 2 * feats), lambda i: (i, 0)),
        ],
        out_shape=[
            jax.ShapeDtypeStruct((nq, feats), BF16),
            jax.ShapeDtypeStruct((nk, 2 * feats), BF16),
        ],
        scratch_shapes=[
            pltpu.VMEM((2, nk, nq), BF16),
            pltpu.VMEM((4, nq), F32),
        ],
        compiler_params=pltpu.CompilerParams(vmem_limit_bytes=48 << 20),
    )(q, qm, da, kv, km, kv, stats)

    lse_each = stats[:, 0:2]
    weight = jax.nn.softmax(lse_each * math.log(2.0), axis=0)
    mine = jnp.take(weight, lax.axis_index("xc"), axis=0)
    o_part = (o.reshape(nq, 2, DH).astype(F32) * mine.T[:, :, None]).reshape(nq, feats).astype(BF16)
    attn = lax.psum_scatter(o_part, "xc", scatter_dimension=0, tiled=True)
    attn = (attn.astype(F32) * valid[:, None]).astype(BF16)
    partial_out = jnp.dot(attn, wo, preferred_element_type=F32).astype(BF16)
    block_out = lax.psum_scatter(partial_out, "head", scatter_dimension=1, tiled=True)
    dwo = lax.psum_scatter(
        jnp.einsum("tf,td->fd", attn, dy_full, preferred_element_type=F32),
        ("z", "xc"),
        scatter_dimension=1,
        tiled=True,
    )
    dq = lax.psum_scatter(dq_part, "xc", scatter_dimension=0, tiled=True)
    dkv = lax.psum_scatter(dkv_part, "z", scatter_dimension=0, tiled=True)
    return (block_out, dq, dkv[:, :feats], dkv[:, feats:], dwo)


def solution(mesh):
    fine = Mesh(mesh.devices.reshape(8, 8, 4), ("z", "xc", "head"))
    seq = ("z", "xc")
    placed = (
        P(seq, "head"),
        P(seq, "head"),
        P(seq, "head"),
        P(seq),
        P("head", None),
        P(seq, "head"),
    )
    return jax.shard_map(
        local,
        mesh=fine,
        in_specs=placed,
        out_specs=(
            P(seq, "head"),
            P(seq, "head"),
            P(seq, "head"),
            P(seq, "head"),
            P("head", seq),
        ),
        check_vma=False,
    )
```

time: 784 us -> 389 us (0.50)
  blocking collectives: 267 us -> 78.8 us
  matrix products: 84.7 us -> 4.55 us
  waiting for transfers between devices: 322 us -> 257 us
  local copies, waits for them, and re-layouts: 66 us -> 11.7 us
  other arithmetic: 25.5 us -> 3.85 us
  Pallas kernels: 0 us -> 16.6 us
    unnamed x1 -> x2, blocking collectives: 254 us -> 25.7 us
    unnamed x6, waiting for transfers between devices: 153 us -> 0.6 us
    reduce_scatter x1 -> x4, waiting for transfers between devices: 22.1 us -> 110 us  [the longest x1 36.1 us: local(): dkv = lax.psum_scatter(dkv_part, 'z', scatter_dimension=0, tiled=True)]
    dot_general x38 -> x3, matrix products: 84.7 us -> 4.55 us  [the longest x1 2.11 us: local(): partial_out = jnp.dot(attn, wo, preferred_element_type=F32).astype(BF16)]
    all_gather x0 -> x3, blocking collectives: none -> 39 us  [the longest x1 13.1 us: local(): da = lax.all_gather(da_own, 'xc', axis=0, tiled=True)]
    reshape x6 -> x0, local copies, waits for them, and re-layouts: 37.7 us -> none  [the longest x1 9.47 us: local(): v_blocks = v_all.reshape(blocks, width, heads, DH)]
    pallas_call x0 -> x2, Pallas kernels: none -> 16.6 us  [the longest x1 9.88 us: local(): pl.pallas_call(backward, grid=(blocks,), in_specs=[whole((nq, feats)), wh...]
    all_gather x2 -> x0, local copies, waits for them, and re-layouts: 13.1 us -> none  [the longest x1 6.58 us: local(): lax.all_gather(key_rows, 'seq', axis=0, tiled=True)]
  transfers between devices with their start and end apart: 5 -> 6, of which waited for: 3 -> 5; matrix products, arithmetic and copies ran while one was open for 7% -> 2% of each run, Pallas kernels for 0% -> 3%
where the time goes in v1:
time: 389 us
  waiting for transfers between devices  257 us (66%)
  blocking collectives  78.8 us (20%)
  Pallas kernels  16.6 us (4%)
  between operations  15.6 us (4%)
  local copies, waits for them, and re-layouts  11.7 us (3%)
  matrix products  4.55 us (1%)
    reduce_scatter x1, waiting for transfers between devices, local(): lax.psum_scatter(jnp.einsum('tf,td->fd', attn, dy_full, preferred_element...  147 us
    reduce_scatter x1, waiting for transfers between devices, local(): dkv = lax.psum_scatter(dkv_part, 'z', scatter_dimension=0, tiled=True)  36.1 us
    reduce_scatter x1, waiting for transfers between devices, local(): dq = lax.psum_scatter(dq_part, 'xc', scatter_dimension=0, tiled=True)  33.9 us
    unnamed x2, blocking collectives  25.7 us
    reduce_scatter x1, waiting for transfers between devices, local(): lax.psum_scatter(partial_out, 'head', scatter_dimension=1, tiled=True)  24.1 us
    reduce_scatter x1, waiting for transfers between devices, local(): attn = lax.psum_scatter(o_part, 'xc', scatter_dimension=0, tiled=True)  15.7 us
    all_gather x1, blocking collectives, local(): dy_full = lax.all_gather(dy, 'head', axis=1, tiled=True)  14 us
    all_gather x1, blocking collectives, local(): da = lax.all_gather(da_own, 'xc', axis=0, tiled=True)  13.1 us
  transfers between devices with their start and end apart: 6, of which 5 were waited for; matrix products, arithmetic and copies ran while one was open for 2% of the time, Pallas kernels for 3%

profile of v1, /device:TPU:8, one launch (start us, length us, event | category | flops | bytes accessed | tf_op | source)
XLA Modules:
  0.0 388.8 jit_solution(4484798703041018805)
XLA Ops:
  7.2 0.0 copy-start
  7.2 0.0 copy-start.18
  7.2 0.0 copy-start.17
  7.2 0.0 copy-start.16
  7.2 0.0 all-gather.2.cloned.1.call-start
  7.3 1.7 pad_maximum_fusion
  8.9 0.0 all-gather.2.cloned.1.call-update
  8.9 0.0 reduce-scatter.6.cloned.1.call-start
  9.0 0.7 compare_convert_fusion
  9.7 14.0 %all_gather.25 = bf16[136,2048]{1,0:T(8,128)(2,1)S(1)} all-gather(bf16[136,512]{1,0:T(8,128)(2,1)} %param.11), channel_id=1, replica_groups=mesh['z'=8,'xc'=8,'head'=4] {'head'}, dimensions={1}, use_global_device_ids=true | all-gather | bytes 696320 | tf_op jit(solution)/shard_map/all_gather | solution.py:95
  23.7 0.0 copy-done.18
  23.7 0.7 dynamic-slice.4
  24.4 0.0 copy-done.17
  24.4 0.6 dynamic-slice.5
  26.3 0.0 copy-done.16
  26.3 0.3 dynamic-update-slice.1
  26.6 0.3 dynamic-update-slice.2
  26.9 9.3 %all-reduce = s32[1088]{0:T(1024)S(1)} all-reduce(s32[1088]{0:T(1024)S(1)} %dynamic-update-slice.1), channel_id=1, replica_groups=mesh['z'=8,'xc'=8,'head'=4] {'xc'}, use_global_device_ids=true, to_apply=%add | all-reduce | flops 1088 | bytes 8704
  36.2 16.4 %all-reduce.1 = s32[1088]{0:T(1024)S(1)} all-reduce(s32[1088]{0:T(1024)S(1)} %dynamic-update-slice.2), channel_id=1, replica_groups=mesh['z'=8,'xc'=8,'head'=4] {'z'}, use_global_device_ids=true, to_apply=%add.1 | all-reduce | flops 1088 | bytes 8704
  52.6 0.0 copy-done
  52.6 0.0 copy-start.13
  52.6 0.5 fusion
  53.1 0.0 copy-done.14
  53.1 13.1 %all_gather.26.da_ref = bf16[1088,256]{1,0:T(8,128)(2,1)S(1)} all-gather(bf16[136,256]{1,0:T(8,128)(2,1)S(1)} %fusion), channel_id=1, replica_groups=mesh['z'=8,'xc'=8,'head'=4] {'xc'}, dimensions={0}, use_global_device_ids=true | all-gather | bytes 626688 | tf_op jit(solution)/shard_map/all_gather | solution.py:99
  66.3 0.0 copy-done.10
  66.3 0.0 copy-done.13
  66.3 13.1 %all_gather.21.q_ref = bf16[1088,256]{1,0:T(8,128)(2,1)S(1)} all-gather(bf16[136,256]{1,0:T(8,128)(2,1)S(1)} %copy-done.13), channel_id=1, replica_groups=mesh['z'=8,'xc'=8,'head'=4] {'xc'}, dimensions={0}, use_global_device_ids=true | all-gather | bytes 626688 | tf_op jit(solution)/shard_map/all_gather | solution.py:92
  79.4 0.2 fusion.4.km_ref
  79.6 0.2 select_convert_fusion.qm_ref
  79.8 0.0 copy-start.3
  79.8 0.0 all-gather.2.cloned.1.call-done.kv_ref.kv_all_ref
  79.9 0.0 copy-start.1
  79.9 1.3 copy-done.1
  81.2 6.7 %shard_map.101 = (bf16[1088,256]{1,0:T(8,128)(2,1)S(1)}, f32[4,8,272]{2,1,0:T(8,128)S(1)}) custom-call(bf16[1088,256]{1,0:T(8,128)(2,1)S(1)} %all_gather.21.q_ref, bf16[1088,128]{1,0:T(8,128)(2,1)S(1)} %select_convert_fusion.qm_ref, bf16[1088,512]{1,0:T(8,128)(2,1)S(1)} %copy-done.1, bf16[1088,128]{1,0:T(8,128)(2,1)S(1)} %fusion.4.km_ref, ...), custom_call_target="tpu_custom_call" | custom-call | tf_op jit(solution)/shard_map/pallas_call | solution.py:114
  87.9 0.8 copy-done.8
  88.8 0.1 all_gather_reshape.3
  88.9 12.8 %all_gather.27.stat_ref = f32[8,4,1088]{2,1,0:T(4,128)S(1)} all-gather(f32[1,4,1088]{2,1,0:T(4,128)S(1)} %all_gather_reshape.3), channel_id=1, replica_groups=mesh['z'=8,'xc'=8,'head'=4] {'xc'}, dimensions={0}, use_global_device_ids=true | all-gather | bytes 156672 | tf_op jit(solution)/shard_map/all_gather | solution.py:135
  101.7 0.1 fusion.7
  101.8 0.2 copy.15
  102.0 0.0 copy-start.9
  102.0 2.5 mul.35
  104.6 0.9 fusion.1
  105.5 0.0 reduce-scatter.6.cloned.1.call-update
  105.5 0.0 reduce-scatter.12.cloned.1.call-start
  105.6 0.4 copy-done.2
  106.0 1.0 copy-done.4
  107.0 0.9 copy-done.6
  107.9 9.9 %shard_map.102 = (bf16[1088,256]{1,0:T(8,128)(2,1)}, bf16[1088,512]{1,0:T(8,128)(2,1)S(1)}) custom-call(bf16[1088,256]{1,0:T(8,128)(2,1)S(1)} %all_gather.21.q_ref, bf16[1088,128]{1,0:T(8,128)(2,1)S(1)} %copy-done.4, bf16[1088,256]{1,0:T(8,128)(2,1)S(1)} %all_gather.26.da_ref, bf16[1088,512]{1,0:T(8,128)(2,1)S(1)} %copy-done.2, ...), custom_call_target="tpu_custom_call" | custom-call | tf_op jit(solution)/shard_map/pallas_call | solution.py:137
  117.8 1.0 copy-done.7
  118.8 0.0 reduce-scatter.12.cloned.1.call-update
  118.8 0.0 reduce-scatter.10.cloned.1.call-start
  118.8 0.5 reduce-scatter.10.cloned.1.call-update
  119.4 0.0 reduce-scatter.8.cloned.1.call-start
  119.4 15.7 %reduce-scatter.6.cloned.1.call-done = bf16[136,256]{1,0:T(8,128)(2,1)} async-done(((bf16[1088,256]{1,0:T(8,128)(2,1)}), bf16[136,256]{1,0:T(8,128)(2,1)}) %reduce-scatter.6.cloned.1.call-update) | async-done | bytes 69648 | tf_op jit(solution)/shard_map/reduce_scatter | solution.py:168
  135.1 2.1 convolution_convert_fusion
  137.2 0.0 reduce-scatter.8.cloned.1.call-update
  137.2 0.0 reduce-scatter.14.cloned.1.call-start
  137.3 1.9 fusion.6
  139.2 0.0 reduce-scatter.14.cloned.1.call-update
  139.3 36.1 %reduce-scatter.12.cloned.1.call-done = bf16[136,512]{1,0:T(8,128)(2,1)} async-done(((bf16[1088,512]{1,0:T(8,128)(2,1)}), bf16[136,512]{1,0:T(8,128)(2,1)}) %reduce-scatter.12.cloned.1.call-update) | async-done | bytes 139280 | tf_op jit(solution)/shard_map/reduce_scatter | solution.py:179
  175.4 1.6 fusion.8
  176.9 33.9 %reduce-scatter.10.cloned.1.call-done = bf16[136,256]{1,0:T(8,128)(2,1)} async-done(((bf16[1088,256]{1,0:T(8,128)(2,1)}), bf16[136,256]{1,0:T(8,128)(2,1)}) %reduce-scatter.10.cloned.1.call-update) | async-done | bytes 69648 | tf_op jit(solution)/shard_map/reduce_scatter | solution.py:178
  210.8 24.1 %reduce-scatter.8.cloned.1.call-done = bf16[136,512]{1,0:T(8,128)(2,1)} async-done(((bf16[136,2048]{1,0:T(8,128)(2,1)}), bf16[136,512]{1,0:T(8,128)(2,1)}) %reduce-scatter.8.cloned.1.call-update) | async-done | bytes 139280 | tf_op jit(solution)/shard_map/reduce_scatter | solution.py:171
  234.9 147.1 %reduce-scatter.14.cloned.1.call-done = f32[256,32]{0,1:T(8,128)} async-done(((f32[256,2048]{0,1:T(8,128)}), f32[256,32]{0,1:T(8,128)}) %reduce-scatter.14.cloned.1.call-update) | async-done | bytes 32784 | tf_op jit(solution)/shard_map/reduce_scatter | solution.py:172
  (25 shorter events, 0.1 us)
Async XLA Ops:
  7.2 45.4 %copy-start = (bf16[256,2048]{1,0:T(8,128)(2,1)S(1)}, bf16[256,2048]{1,0:T(8,128)(2,1)}, u32[]{:S(2)}) copy-start(bf16[256,2048]{1,0:T(8,128)(2,1)} %param.10) | copy-start | bytes 3145732
  7.2 16.5 %copy-start.18 = (u32[256]{0:T(256)S(1)}, u32[256]{0:T(256)}, u32[]{:S(2)}) copy-start(u32[256]{0:T(256)} %constant.65) | copy-start | bytes 3076
  7.2 17.2 %copy-start.17 = (u32[256]{0:T(256)S(1)}, u32[256]{0:T(256)}, u32[]{:S(2)}) copy-start(u32[256]{0:T(256)} %constant.70) | copy-start | bytes 3076
  7.2 19.1 %copy-start.16 = (s32[136]{0:T(256)S(1)}, s32[136]{0:T(256)}, u32[]{:S(2)}) copy-start(s32[136]{0:T(256)} %param.9) | copy-start | bytes 1636
  7.2 72.6 %all-gather.2.cloned.1.call-start = ((), (), s32[]{:S(2)}) async-start(), calls=%async_computation.5 | async-start | bytes 1253376 | tf_op jit(solution)/shard_map/all_gather | solution.py:91
  8.9 126.1 %reduce-scatter.6.cloned.1.call-start = ((), (), s32[]{:S(2)}) async-start(), calls=%async_computation.6 | async-start | bytes 626688 | tf_op jit(solution)/shard_map/reduce_scatter | solution.py:168
  9.7 43.4 %copy-start.14 = (f32[136]{0:T(256)}, f32[136]{0:T(256)S(1)}, u32[]{:S(2)}) copy-start(f32[136]{0:T(256)S(1)} %compare_convert_fusion) | copy-start | bytes 1636
  23.7 42.6 %copy-start.10 = (bf16[136,2048]{1,0:T(8,128)(2,1)}, bf16[136,2048]{1,0:T(8,128)(2,1)S(1)}, u32[]{:S(2)}) copy-start(bf16[136,2048]{1,0:T(8,128)(2,1)S(1)} %all_gather.25) | copy-start | bytes 1671172
  52.6 13.7 %copy-start.13 = (bf16[136,256]{1,0:T(8,128)(2,1)S(1)}, bf16[136,256]{1,0:T(8,128)(2,1)}, u32[]{:S(2)}) copy-start(bf16[136,256]{1,0:T(8,128)(2,1)} %param.6) | copy-start | bytes 208900
  79.8 8.1 %copy-start.3 = (bf16[1088,128]{1,0:T(8,128)(2,1)}, bf16[1088,128]{1,0:T(8,128)(2,1)S(1)}, u32[]{:S(2)}) copy-start(bf16[1088,128]{1,0:T(8,128)(2,1)S(1)} %select_convert_fusion.qm_ref) | copy-start | bytes 835588
  79.9 1.3 copy-start.1
  87.9 0.8 copy-start.8
  101.6 2.9 copy-start.5
  102.0 2.6 copy-start.9
  104.6 1.5 copy-start.2
  105.5 69.8 %reduce-scatter.12.cloned.1.call-start = ((), (), s32[]{:S(2)}) async-start(), calls=%async_computation.9 | async-start | bytes 1253376 | tf_op jit(solution)/shard_map/reduce_scatter | solution.py:179
  106.0 1.0 copy-start.4
  107.0 0.9 copy-start.6
  117.8 1.0 copy-start.7
  118.8 16.3 %copy-start.15 = (f32[136]{0:T(256)S(1)}, f32[136]{0:T(256)}, u32[]{:S(2)}) copy-start(f32[136]{0:T(256)} %copy-done.14) | copy-start | bytes 1636
  118.8 92.0 %reduce-scatter.10.cloned.1.call-start = ((), (), s32[]{:S(2)}) async-start(), calls=%async_computation.8 | async-start | bytes 626688 | tf_op jit(solution)/shard_map/reduce_scatter | solution.py:178
  119.4 17.9 %copy-start.11 = (bf16[136,2048]{1,0:T(8,128)(2,1)S(1)}, bf16[136,2048]{1,0:T(8,128)(2,1)}, u32[]{:S(2)}) copy-start(bf16[136,2048]{1,0:T(8,128)(2,1)} %copy-done.10) | copy-start | bytes 1671172
  119.4 115.5 %reduce-scatter.8.cloned.1.call-start = ((), (), s32[]{:S(2)}) async-start(), calls=%async_computation.7 | async-start | bytes 696320 | tf_op jit(solution)/shard_map/reduce_scatter | solution.py:171
  135.1 2.2 copy-start.12
  137.2 244.8 %reduce-scatter.14.cloned.1.call-start = ((), (), s32[]{:S(2)}) async-start(), calls=%async_computation.10 | async-start | bytes 2129920 | tf_op jit(solution)/shard_map/reduce_scatter | solution.py:172
Sparse Core Ops, SparseCore 0:
  10.4 41.5 all-gather.1
  105.7 29.3 reduce-scatter.5
  137.6 37.6 reduce-scatter.11
  178.5 32.2 reduce-scatter.9
  213.9 20.8 reduce-scatter.7
  239.4 142.5 reduce-scatter.13
